TPU v7x, 32 devices: a whole 2x2x4 slice. The times are simulated.
32 devices in a mesh: lag: 16 (over z, y, x), par: 2 (over core).
Axes of the slice: x: 2, y: 2, z: 4, core: 2. Of those that a mesh axis runs over, the one named last changes fastest.
Arguments:
- prior_rows: bfloat16 [16, 512, 4096], P('lag', None, 'par'), may hold values from -0.125 to 0.125
- raw_rows: bfloat16 [16, 512, 4096], P('lag', None, 'par'), may hold values from -6 to 6
Outputs:
- diag_zero: float32 [16, 512, 512], P('lag', 'par')
- diag_one: float32 [16, 512, 512], P('lag', 'par')
All inputs are finite; a program needn't handle non-finite values.
Results may differ from a plain program's by a relative error of at most 0.0003.
Values may be sent and summed in bfloat16 or wider, within the bound.
A program may use at most 64 MiB of HBM per device.

v0:
```python
import jax
import jax.numpy as jnp
from jax import lax
from jax.sharding import PartitionSpec as P


def passed_along(block, axis, distance):
    devices = range(lax.axis_size(axis))
    route = [(i - distance, i) for i in devices if i - distance in devices]
    return lax.ppermute(block, axis, route)


def carried_in(part, axis, combine, identity):
    place = lax.axis_index(axis)
    gathered = lax.all_gather(part, axis)
    state = jnp.zeros_like(part) + jnp.asarray(identity, part.dtype)

    def one(turn, state):
        return combine(state, lax.dynamic_index_in_dim(gathered, turn, 0, False))

    return lax.fori_loop(0, place, one, state)


def add_terms(earlier_term, later_term):
    return earlier_term + later_term


def body(prior_rows, raw_rows):
    incoming = passed_along(raw_rows, "lag", -1)
    following = jnp.concatenate([raw_rows[1:], incoming], axis=0)
    offset_zero = jnp.einsum(
        "lsp,ltp->lst", prior_rows, raw_rows, preferred_element_type=jnp.float32
    )
    offset_one = jnp.einsum(
        "lsp,ltp->lst", prior_rows, following, preferred_element_type=jnp.float32
    )
    stacked = jnp.stack([offset_zero, offset_one], axis=0)
    shares = lax.psum_scatter(stacked, "par", scatter_dimension=2, tiled=True)
    running = jnp.cumsum(shares, axis=1)
    totals = running[:, -1]
    earlier = carried_in(totals, "lag", add_terms, jnp.zeros_like(totals))
    result = running + earlier[:, None]
    return (result[0], result[1])


def solution(mesh):
    in_specs = (P("lag", None, "par"), P("lag", None, "par"))
    out_specs = (P("lag", "par", None), P("lag", "par", None))
    return jax.shard_map(body, mesh=mesh, in_specs=in_specs, out_specs=out_specs, check_vma=False)
```

profile of v0, /device:TPU:24, one launch (start us, length us, event | category | flops | bytes accessed | tf_op | source)
XLA Modules:
  0.0 293.0 jit_solution(16033226472213250084)
XLA Ops:
  7.2 0.0 copy-start
  7.2 0.0 reduce-scatter.2.cloned.1.call-start
  7.2 4.4 %collective-permute-start = (bf16[1,512,2048]{2,1,0:T(8,128)(2,1)}, bf16[1,512,2048]{2,1,0:T(8,128)(2,1)S(1)}, u32[]{:S(2)}, u32[]{:S(2)}) collective-permute-start(bf16[1,512,2048]{2,1,0:T(8,128)(2,1)} %param.5), channel_id=1, source_target_pairs={{2,0},{4,2},{6,4},{8,6},{10,8},{12,10},{14,12},{16,14},{18,16},{20... | collective-permute-start | bytes 6291464 | tf_op jit(solution)/shard_map/ppermute | solution.py:10
  11.6 0.0 copy-done
  11.6 2.9 fusion.6
  14.5 42.3 %collective-permute-done = bf16[1,512,2048]{2,1,0:T(8,128)(2,1)S(1)} collective-permute-done((bf16[1,512,2048]{2,1,0:T(8,128)(2,1)}, bf16[1,512,2048]{2,1,0:T(8,128)(2,1)S(1)}, u32[]{:S(2)}, u32[]{:S(2)}) %collective-permute-start) | collective-permute-done | bytes 2097184 | tf_op jit(solution)/shard_map/ppermute | solution.py:10
  56.8 1.3 fusion.11
  58.1 1.5 pad_maximum_fusion
  59.6 0.0 reduce-scatter.2.cloned.1.call-update
  59.7 0.0 all-gather.3.cloned.1.call-start
  59.7 11.7 %reduce-scatter.2.cloned.1.call-done = f32[2,1,256,512]{3,2,1,0:T(8,128)} async-done(((f32[2,1,512,512]{3,2,1,0:T(8,128)}), f32[2,1,256,512]{3,2,1,0:T(8,128)}) %reduce-scatter.2.cloned.1.call-update) | async-done | bytes 1048592 | tf_op jit(solution)/shard_map/reduce_scatter | solution.py:38
  71.5 0.0 all-gather.3.cloned.1.call-update
  71.5 193.7 %all-gather.3.cloned.1.call-done = f32[32,1,256,512]{3,2,1,0:T(8,128)} async-done(((f32[2,1,256,512]{3,2,1,0:T(8,128)}), f32[32,1,256,512]{3,2,1,0:T(8,128)}) %all-gather.3.cloned.1.call-update) | async-done | bytes 16777232 | tf_op jit(solution)/shard_map/all_gather | solution.py:15
  265.2 0.1 broadcast_in_dim.6
  265.3 18.3 %while.10 = (s32[]{:T(128)}, f32[2,256,512]{2,1,0:T(8,128)S(1)}, s32[]{:T(128)}, f32[16,2,256,512]{3,2,1,0:T(8,128)}, s32[]{:T(128)}, /*index=5*/s32[]{:T(128)}, s32[]{:T(128)}) while((s32[]{:T(128)}, f32[2,256,512]{2,1,0:T(8,128)S(1)}, s32[]{:T(128)}, f32[16,2,256,512]{3,2,1,0:T(8,128)}, s32[]{:T(128)}, /*index=5*/s32[]{:T(128)}, ...), condition=%wide.region_2.3_spmd, body=%wide.region_1.0_spmd.sunk | while | flops 262149 | bytes 3145851 | solution.py:21
  265.4 1.5 bitcast_add_fusion.3
  266.9 1.5 bitcast_add_fusion.3
  268.4 1.5 bitcast_add_fusion.3
  269.9 1.5 bitcast_add_fusion.3
  271.5 1.5 bitcast_add_fusion.3
  273.0 1.5 bitcast_add_fusion.3
  274.5 1.5 bitcast_add_fusion.3
  276.1 1.5 bitcast_add_fusion.3
  277.6 1.5 bitcast_add_fusion.3
  279.1 1.5 bitcast_add_fusion.3
  280.6 1.5 bitcast_add_fusion.3
  282.2 1.5 bitcast_add_fusion.3
  283.7 1.4 bitcast_add_fusion.1
  285.1 1.0 slice_bitcast_fusion
Async XLA Ops:
  7.2 4.4 %copy-start = (bf16[1,512,2048]{2,1,0:T(8,128)(2,1)S(1)}, bf16[1,512,2048]{2,1,0:T(8,128)(2,1)}, u32[]{:S(2)}) copy-start(bf16[1,512,2048]{2,1,0:T(8,128)(2,1)} %param.4) | copy-start | bytes 6291460
  7.2 64.3 %reduce-scatter.2.cloned.1.call-start = ((), (), s32[]{:S(2)}) async-start(), calls=%async_computation.1 | async-start | bytes 3145728 | tf_op jit(solution)/shard_map/reduce_scatter | solution.py:38
  7.2 49.6 %collective-permute-start = (bf16[1,512,2048]{2,1,0:T(8,128)(2,1)}, bf16[1,512,2048]{2,1,0:T(8,128)(2,1)S(1)}, u32[]{:S(2)}, u32[]{:S(2)}) collective-permute-start(bf16[1,512,2048]{2,1,0:T(8,128)(2,1)} %param.5), channel_id=1, source_target_pairs={{2,0},{4,2},{6,4},{8,6},{10,8},{12,10},{14,12},{16,14},{18,16},{20... | collective-permute-start | bytes 6291464 | tf_op jit(solution)/shard_map/ppermute | solution.py:10
  59.7 205.6 %all-gather.3.cloned.1.call-start = ((), (), s32[]{:S(2)}) async-start(), calls=%async_computation.2 | async-start | bytes 17825792 | tf_op jit(solution)/shard_map/all_gather | solution.py:15
Sparse Core Ops, SparseCore 0:
  59.8 11.6 reduce-scatter.1
  74.6 190.5 all-gather.2
where the time goes:
time: 298 us; the launch traced here: 293 us
  waiting for transfers between devices  248 us (83%)
  other arithmetic  21 us (7%)
  between operations  14.1 us (5%)
  starting transfers between devices  4.45 us (1%)
  matrix products  4.16 us (1%)
    all_gather x1, waiting for transfers between devices, carried_in(): gathered = lax.all_gather(part, axis)  194 us
    ppermute x1, waiting for transfers between devices, passed_along(): return lax.ppermute(block, axis, route)  42.3 us
    add x12, other arithmetic, add_terms(): return earlier_term + later_term  18.1 us
    reduce_scatter x1, waiting for transfers between devices, body(): shares = lax.psum_scatter(stacked, 'par', scatter_dimension=2, tiled=True)  11.7 us
  transfers between devices with their start and end apart: 3, of which 3 were waited for; matrix products, arithmetic and copies ran while one was open for 1% of the time, Pallas kernels for 0%

commit v1 on v0

v1 whole, which is shorter than its diff:
```python
import functools

import jax
import jax.numpy as jnp
from jax import lax
from jax.experimental import pallas as pl
from jax.experimental.pallas import tpu as pltpu
from jax.sharding import PartitionSpec as P

MESH = pl.DeviceIdType.MESH
SENT = jnp.float32


def group_size(lags, rows):
    best = 1
    for size in range(1, lags + 1):
        if lags % size == 0 and size * size <= lags and rows % (16 * size) == 0:
            best = size
    return best


def kernel(
    lags, pars, members, zero_items, one_items,
    prior_hbm, raw_hbm, zero_out, one_out,
    prior, raw, coming,
    zero_part, zero_met, zero_tile, zero_mates, zero_groups, zero_ahead, zero_first, zero_back,
    one_part, one_met, one_tile, one_mates, one_groups, one_ahead, one_first, one_back,
    load_sem, shift_send, shift_recv,
    zero_sems, one_sems,
):
    lag = lax.axis_index("lag")
    par = lax.axis_index("par")
    groups = lags // members
    group = lag // members
    member = lax.rem(lag, members)
    base = group * members

    loads = [
        pltpu.make_async_copy(prior_hbm.at[0], prior, load_sem.at[0]),
        pltpu.make_async_copy(raw_hbm.at[0], raw, load_sem.at[1]),
    ]
    for load in loads:
        load.start()

    barrier = pltpu.get_barrier_semaphore()

    def greet(other_lag, other_par):
        pl.semaphore_signal(barrier, inc=1, device_id=(other_lag, other_par), device_id_type=MESH)

    for step in range(1, pars):
        greet(lag, lax.rem(par + step, pars))
    for step in range(1, members):
        greet(base + lax.rem(member + step, members), par)
    for step in range(1, groups):
        greet(lax.rem(group + step, groups) * members + member, par)

    @pl.when(lag > 0)
    def _():
        greet(lag - 1, par)

    @pl.when(lag < lags - 1)
    def _():
        greet(lag + 1, par)

    fixed = (pars - 1) + (members - 1) + (groups - 1)
    pl.semaphore_wait(barrier, fixed + jnp.minimum(lag, 1) + jnp.minimum(lags - 1 - lag, 1))

    span = raw.shape[0] // one_items

    def shift(item):
        rows = pl.ds(item * span, span)
        return pltpu.make_async_remote_copy(
            src_ref=raw_hbm.at[0, rows],
            dst_ref=coming.at[rows],
            send_sem=shift_send.at[item],
            recv_sem=shift_recv.at[item],
            device_id=(lag - 1, par),
            device_id_type=MESH,
        )

    @pl.when(lag > 0)
    def _():
        for item in range(one_items):
            shift(item).start()

    def lag_sums(item, rows_ref, out_ref, part, met, tile, mates, totals, ahead, first, back, sems):
        (part_send, part_recv, mate_send, mate_recv, group_send, group_recv, back_send, back_recv) = sems
        pending = []
        width = part.shape[-1]
        share = part.shape[2]
        quarter = tile.shape[2]
        columns = pl.ds(item * width, width)
        product = lax.dot_general(
            prior[...], rows_ref[columns, :], (((1,), (1,)), ((), ())),
            preferred_element_type=jnp.float32,
        )
        for owner in range(pars):
            part[item, owner] = product[owner * share:(owner + 1) * share]

        def to_peer(step):
            peer = lax.rem(par + step, pars)
            return pltpu.make_async_remote_copy(
                src_ref=part.at[item, peer],
                dst_ref=met.at[item, step - 1],
                send_sem=part_send.at[item, step - 1],
                recv_sem=part_recv.at[item, step - 1],
                device_id=(lag, peer),
                device_id_type=MESH,
            )

        for step in range(1, pars):
            copy = to_peer(step)
            copy.start()
            pending.append(copy)
        total = part[item, par]
        for step in range(1, pars):
            to_peer(step).wait_recv()
            total = total + met[item, step - 1]
        for owner in range(members):
            tile[item, owner] = total[owner * quarter:(owner + 1) * quarter]

        def to_mate(step):
            mate = lax.rem(member + step, members)
            return pltpu.make_async_remote_copy(
                src_ref=tile.at[item, mate],
                dst_ref=mates.at[item, member],
                send_sem=mate_send.at[item, mate],
                recv_sem=mate_recv.at[item, member],
                device_id=(base + mate, par),
                device_id_type=MESH,
            )

        def from_mate(step):
            mate = lax.rem(member + step, members)
            return pltpu.make_async_remote_copy(
                src_ref=tile.at[item, mate],
                dst_ref=mates.at[item, mate],
                send_sem=mate_send.at[item, mate],
                recv_sem=mate_recv.at[item, mate],
                device_id=(base + mate, par),
                device_id_type=MESH,
            )

        for step in range(1, members):
            copy = to_mate(step)
            copy.start()
            pending.append(copy)
        mates[item, member] = tile[item, member]
        for step in range(1, members):
            from_mate(step).wait_recv()

        total = mates[item, 0]
        for mate in range(1, members):
            total = total + mates[item, mate]
        totals[item] = total

        def to_group(step):
            return pltpu.make_async_remote_copy(
                src_ref=totals.at[item],
                dst_ref=ahead.at[item, step - 1],
                send_sem=group_send.at[item, step - 1],
                recv_sem=group_recv.at[item, step - 1],
                device_id=((group + step) * members + member, par),
                device_id_type=MESH,
            )

        for step in range(1, groups):
            @pl.when(group + step < groups)
            def _():
                to_group(step).start()

        first[item, 0] = jnp.zeros_like(total)
        for step in range(1, groups):
            @pl.when(group >= step)
            def _():
                to_group(step).wait_recv()
                first[item, 0] += ahead[item, step - 1]
        for mate in range(1, members):
            first[item, mate] = first[item, mate - 1] + mates[item, mate - 1]

        def to_member(step):
            mate = lax.rem(member + step, members)
            return pltpu.make_async_remote_copy(
                src_ref=first.at[item, mate],
                dst_ref=back.at[item, member],
                send_sem=back_send.at[item, mate],
                recv_sem=back_recv.at[item, member],
                device_id=(base + mate, par),
                device_id_type=MESH,
            )

        def from_member(step):
            mate = lax.rem(member + step, members)
            return pltpu.make_async_remote_copy(
                src_ref=first.at[item, mate],
                dst_ref=back.at[item, mate],
                send_sem=back_send.at[item, mate],
                recv_sem=back_recv.at[item, mate],
                device_id=(base + mate, par),
                device_id_type=MESH,
            )

        for step in range(1, members):
            copy = to_member(step)
            copy.start()
            pending.append(copy)
        back[item, member] = first[item, member]
        for step in range(1, members):
            from_member(step).wait_recv()
        for owner in range(members):
            out_ref[0, owner * quarter:(owner + 1) * quarter, item * width:(item + 1) * width] = (
                back[item, owner] + tile[item, owner]
            )

        def finish():
            for copy in pending:
                copy.wait_send()
            for step in range(1, groups):
                @pl.when(group + step < groups)
                def _():
                    to_group(step).wait_send()

        return finish

    for load in loads:
        load.wait()
    ends = []
    for item in range(zero_items):
        ends.append(lag_sums(
            item, raw, zero_out, zero_part, zero_met, zero_tile, zero_mates,
            zero_groups, zero_ahead, zero_first, zero_back, zero_sems,
        ))
    for item in range(one_items):
        @pl.when(lag < lags - 1)
        def _():
            shift(item).wait_recv()

        @pl.when(lag == lags - 1)
        def _():
            rows = pl.ds(item * span, span)
            coming[rows, :] = jnp.zeros((span, coming.shape[1]), coming.dtype)

        ends.append(lag_sums(
            item, coming, one_out, one_part, one_met, one_tile, one_mates,
            one_groups, one_ahead, one_first, one_back, one_sems,
        ))
    for end in ends:
        end()

    @pl.when(lag > 0)
    def _():
        for item in range(one_items):
            shift(item).wait_send()


def scratch_of(items, lags, pars, members, sensors):
    width, share = sensors // items, sensors // pars
    quarter, groups = share // members, lags // members
    f32 = jnp.float32
    buffers = [
        pltpu.VMEM((items, pars, share, width), f32),
        pltpu.VMEM((items, max(pars - 1, 1), share, width), f32),
        pltpu.VMEM((items, members, quarter, width), f32),
        pltpu.VMEM((items, members, quarter, width), f32),
        pltpu.VMEM((items, quarter, width), f32),
        pltpu.VMEM((items, max(groups - 1, 1), quarter, width), f32),
        pltpu.VMEM((items, members, quarter, width), f32),
        pltpu.VMEM((items, members, quarter, width), f32),
    ]
    counts = (pars, pars, members, members, groups, groups, members, members)
    return buffers, tuple(pltpu.SemaphoreType.DMA((items, count)) for count in counts)


def solution(mesh):
    lags, pars = mesh.shape["lag"], mesh.shape["par"]

    def body(prior_rows, raw_rows):
        sensors, panel = prior_rows.shape[1:]
        share = sensors // pars
        members = group_size(lags, share)
        zero_items, one_items = 1, 4
        zero_buffers, zero_sems = scratch_of(zero_items, lags, pars, members, sensors)
        one_buffers, one_sems = scratch_of(one_items, lags, pars, members, sensors)
        out = jax.ShapeDtypeStruct((1, share, sensors), jnp.float32)
        return pl.pallas_call(
            functools.partial(kernel, lags, pars, members, zero_items, one_items),
            out_shape=(out, out),
            in_specs=[pl.BlockSpec(memory_space=pl.ANY)] * 2,
            out_specs=[pl.BlockSpec(memory_space=pltpu.VMEM)] * 2,
            scratch_shapes=[
                pltpu.VMEM((sensors, panel), jnp.bfloat16),
                pltpu.VMEM((sensors, panel), jnp.bfloat16),
                pltpu.VMEM((sensors, panel), jnp.bfloat16),
                *zero_buffers,
                *one_buffers,
                pltpu.SemaphoreType.DMA((2,)),
                pltpu.SemaphoreType.DMA((one_items,)),
                pltpu.SemaphoreType.DMA((one_items,)),
                zero_sems,
                one_sems,
            ],
            compiler_params=pltpu.CompilerParams(
                collective_id=0, has_side_effects=True, vmem_limit_bytes=48 * 2**20
            ),
            cost_estimate=pl.CostEstimate(
                flops=4 * sensors * sensors * panel,
                bytes_accessed=4 * sensors * panel + 8 * share * sensors,
                transcendentals=0,
            ),
        )(prior_rows, raw_rows)

    in_specs = (P("lag", None, "par"), P("lag", None, "par"))
    out_specs = (P("lag", "par", None), P("lag", "par", None))
    return jax.shard_map(body, mesh=mesh, in_specs=in_specs, out_specs=out_specs, check_vma=False)
```

time: 298 us -> 121 us (0.41); the launches traced: 293 us -> 121 us
  waiting for transfers between devices: 248 us -> 0 us
  Pallas kernels: 0 us -> 115 us
  other arithmetic: 21 us -> 0 us
  between operations: 14.1 us -> 0.65 us
  starting transfers between devices: 4.45 us -> 0 us
  matrix products: 4.16 us -> 0 us
  local copies, waits for them, and re-layouts: 1.16 us -> 4.76 us
    all_gather x1 -> x0, waiting for transfers between devices: 194 us -> none  [carried_in(): gathered = lax.all_gather(part, axis)]
    pallas_call x0 -> x1, Pallas kernels: none -> 115 us  [body(): pl.pallas_call(functools.partial(kernel, lags, pars, members, zero_items,...]
    ppermute x1 -> x0, waiting for transfers between devices: 42.3 us -> none  [passed_along(): return lax.ppermute(block, axis, route)]
    add x13 -> x0, other arithmetic: 19.5 us -> none  [the longest x12 18.1 us: add_terms(): return earlier_term + later_term]
    reduce_scatter x1 -> x0, waiting for transfers between devices: 11.7 us -> none  [body(): shares = lax.psum_scatter(stacked, 'par', scatter_dimension=2, tiled=True)]
    unnamed x2 -> x6, local copies, waits for them, and re-layouts: 0.01 us -> 4.76 us
    ppermute x1 -> x0, starting transfers between devices: 4.37 us -> none  [passed_along(): return lax.ppermute(block, axis, route)]
    dot_general x2 -> x0, matrix products: 4.16 us -> none  [the longest x1 2.87 us: body(): jnp.einsum('lsp,ltp->lst', prior_rows, raw_rows, preferred_element_type=j...]
  transfers between devices with their start and end apart: 3 -> 0, of which waited for: 3 -> 0; matrix products, arithmetic and copies ran while one was open for 1% -> 0% of each run, Pallas kernels for 0% -> 0%
where the time goes in v1:
time: 121 us
  Pallas kernels  115 us (95%)
  local copies, waits for them, and re-layouts  4.76 us (4%)
    pallas_call x1, Pallas kernels, body(): pl.pallas_call(functools.partial(kernel, lags, pars, members, zero_items,...  115 us
    unnamed x6, local copies, waits for them, and re-layouts  4.76 us

profile of v1, /device:TPU:24, one launch (start us, length us, event | category | flops | bytes accessed | tf_op | source)
XLA Modules:
  0.0 120.6 jit_solution(2927152357424879472)
XLA Ops:
  0.6 0.0 copy-start
  0.6 1.6 %copy-done = bf16[1,512,2048]{2,1,0:T(8,128)(2,1)S(1)} copy-done((bf16[1,512,2048]{2,1,0:T(8,128)(2,1)S(1)}, bf16[1,512,2048]{2,1,0:T(8,128)(2,1)}, u32[]{:S(2)}) %copy-start) | copy-done | bytes 2097176
  2.2 0.0 copy-start.1
  2.2 1.6 %copy-done.1 = bf16[1,512,2048]{2,1,0:T(8,128)(2,1)S(1)} copy-done((bf16[1,512,2048]{2,1,0:T(8,128)(2,1)S(1)}, bf16[1,512,2048]{2,1,0:T(8,128)(2,1)}, u32[]{:S(2)}) %copy-start.1) | copy-done | bytes 2097176
  3.8 115.2 %shard_map.41 = (f32[1,256,512]{2,1,0:T(8,128)S(1)}, f32[1,256,512]{2,1,0:T(8,128)S(1)}) custom-call(bf16[1,512,2048]{2,1,0:T(8,128)(2,1)S(1)} %copy-done, bf16[1,512,2048]{2,1,0:T(8,128)(2,1)S(1)} %copy-done.1), custom_call_target="tpu_custom_call" | custom-call | flops 2147483648 | bytes 5242880 | tf_op jit(solution)/shard_map/pallas_call | solution.py:285
  119.0 0.8 copy.6
  119.8 0.8 copy.7
Async XLA Ops:
  0.6 1.6 %copy-start = (bf16[1,512,2048]{2,1,0:T(8,128)(2,1)S(1)}, bf16[1,512,2048]{2,1,0:T(8,128)(2,1)}, u32[]{:S(2)}) copy-start(bf16[1,512,2048]{2,1,0:T(8,128)(2,1)} %prior_hbm.1) | copy-start | bytes 6291460
  2.2 1.6 %copy-start.1 = (bf16[1,512,2048]{2,1,0:T(8,128)(2,1)S(1)}, bf16[1,512,2048]{2,1,0:T(8,128)(2,1)}, u32[]{:S(2)}) copy-start(bf16[1,512,2048]{2,1,0:T(8,128)(2,1)} %raw_hbm.1) | copy-start | bytes 6291460

commit v2 on v1

v2 whole, which is shorter than its diff:
```python
import functools

import jax
import jax.numpy as jnp
from jax import lax
from jax.experimental import pallas as pl
from jax.experimental.pallas import tpu as pltpu
from jax.sharding import PartitionSpec as P

MESH = pl.DeviceIdType.MESH
SENT = jnp.float32


def group_size(lags, rows):
    best = 1
    for size in range(1, lags + 1):
        if lags % size == 0 and size * size <= lags and rows % (16 * size) == 0:
            best = size
    return best


def kernel(
    lags, pars, members, one_items,
    prior_hbm, raw_hbm, zero_out, one_out,
    prior, raw, coming,
    zero_part, zero_met, zero_tile, zero_mates, zero_groups, zero_ahead, zero_first, zero_back,
    one_part, one_met, one_tile, one_mates, one_groups, one_ahead, one_first, one_back,
    load_sem, shift_send, shift_recv,
    zero_sems, one_sems,
):
    lag = lax.axis_index("lag")
    par = lax.axis_index("par")
    groups = lags // members
    group = lag // members
    member = lax.rem(lag, members)
    base = group * members

    loads = [
        pltpu.make_async_copy(prior_hbm.at[0], prior, load_sem.at[0]),
        pltpu.make_async_copy(raw_hbm.at[0], raw, load_sem.at[1]),
    ]
    for load in loads:
        load.start()

    barrier = pltpu.get_barrier_semaphore()

    def greet(other_lag, other_par):
        pl.semaphore_signal(barrier, inc=1, device_id=(other_lag, other_par), device_id_type=MESH)

    for step in range(1, pars):
        greet(lag, lax.rem(par + step, pars))
    for step in range(1, members):
        greet(base + lax.rem(member + step, members), par)
    for step in range(1, groups):
        greet(lax.rem(group + step, groups) * members + member, par)

    @pl.when(lag > 0)
    def _():
        greet(lag - 1, par)

    @pl.when(lag < lags - 1)
    def _():
        greet(lag + 1, par)

    fixed = (pars - 1) + (members - 1) + (groups - 1)
    pl.semaphore_wait(barrier, fixed + jnp.minimum(lag, 1) + jnp.minimum(lags - 1 - lag, 1))

    span = raw.shape[0] // one_items

    def shift(item):
        rows = pl.ds(item * span, span)
        return pltpu.make_async_remote_copy(
            src_ref=raw_hbm.at[0, rows],
            dst_ref=coming.at[rows],
            send_sem=shift_send.at[item],
            recv_sem=shift_recv.at[item],
            device_id=(lag - 1, par),
            device_id_type=MESH,
        )

    def stages_of(item, rows_ref, out_ref, part, met, tile, mates, totals, ahead, first, back, sems):
        (part_send, part_recv, mate_send, mate_recv, group_send, group_recv, back_send, back_recv) = sems
        width = part.shape[-1]
        share = part.shape[2]
        quarter = tile.shape[2]

        def to_peer(step):
            peer = lax.rem(par + step, pars)
            return pltpu.make_async_remote_copy(
                src_ref=part.at[item, peer],
                dst_ref=met.at[item, step - 1],
                send_sem=part_send.at[item, step - 1],
                recv_sem=part_recv.at[item, step - 1],
                device_id=(lag, peer),
                device_id_type=MESH,
            )

        def among(source, target, send_sem, recv_sem, step, incoming):
            mate = lax.rem(member + step, members)
            place = mate if incoming else member
            return pltpu.make_async_remote_copy(
                src_ref=source.at[item, mate],
                dst_ref=target.at[item, place],
                send_sem=send_sem.at[item, mate],
                recv_sem=recv_sem.at[item, place],
                device_id=(base + mate, par),
                device_id_type=MESH,
            )

        gather = functools.partial(among, tile, mates, mate_send, mate_recv)
        give = functools.partial(among, first, back, back_send, back_recv)

        def to_group(step):
            return pltpu.make_async_remote_copy(
                src_ref=totals.at[item],
                dst_ref=ahead.at[item, step - 1],
                send_sem=group_send.at[item, step - 1],
                recv_sem=group_recv.at[item, step - 1],
                device_id=((group + step) * members + member, par),
                device_id_type=MESH,
            )

        def multiply():
            product = lax.dot_general(
                prior[...], rows_ref[pl.ds(item * width, width), :], (((1,), (1,)), ((), ())),
                preferred_element_type=jnp.float32,
            )
            for owner in range(pars):
                part[item, owner] = product[owner * share:(owner + 1) * share]
            for step in range(1, pars):
                to_peer(step).start()

        def sum_peers():
            total = part[item, par]
            for step in range(1, pars):
                to_peer(step).wait_recv()
                total = total + met[item, step - 1]
            for owner in range(members):
                tile[item, owner] = total[owner * quarter:(owner + 1) * quarter]
            for step in range(1, members):
                gather(step, False).start()
            mates[item, member] = tile[item, member]

        def sum_group():
            for step in range(1, members):
                gather(step, True).wait_recv()
            total = mates[item, 0]
            for mate in range(1, members):
                total = total + mates[item, mate]
            totals[item] = total
            for step in range(1, groups):
                @pl.when(group + step < groups)
                def _():
                    to_group(step).start()

        def sum_before():
            first[item, 0] = jnp.zeros_like(totals[item])
            for step in range(1, groups):
                @pl.when(group >= step)
                def _():
                    to_group(step).wait_recv()
                    first[item, 0] += ahead[item, step - 1]
            for mate in range(1, members):
                first[item, mate] = first[item, mate - 1] + mates[item, mate - 1]
            for step in range(1, members):
                give(step, False).start()
            back[item, member] = first[item, member]

        def store():
            for step in range(1, members):
                give(step, True).wait_recv()
            for owner in range(members):
                out_ref[0, owner * quarter:(owner + 1) * quarter, item * width:(item + 1) * width] = (
                    back[item, owner] + tile[item, owner]
                )

        def finish():
            for step in range(1, pars):
                to_peer(step).wait_send()
            for step in range(1, members):
                gather(step, False).wait_send()
                give(step, False).wait_send()
            for step in range(1, groups):
                @pl.when(group + step < groups)
                def _():
                    to_group(step).wait_send()

        return multiply, sum_peers, sum_group, sum_before, store, finish

    def arrive(item):
        @pl.when(lag < lags - 1)
        def _():
            shift(item).wait_recv()

        @pl.when(lag == lags - 1)
        def _():
            rows = pl.ds(item * span, span)
            coming[rows, :] = jnp.zeros((span, coming.shape[1]), coming.dtype)

    def depart(item):
        @pl.when(lag > 0)
        def _():
            shift(item).start()

    zero = stages_of(
        0, raw, zero_out, zero_part, zero_met, zero_tile, zero_mates,
        zero_groups, zero_ahead, zero_first, zero_back, zero_sems,
    )
    ones = [
        stages_of(
            item, coming, one_out, one_part, one_met, one_tile, one_mates,
            one_groups, one_ahead, one_first, one_back, one_sems,
        )
        for item in range(one_items)
    ]
    lines = [zero] + ones

    depart(0)
    depart(1)
    for load in loads:
        load.wait()
    for turn, line in enumerate(lines):
        if turn >= 1:
            arrive(turn - 1)
        line[0]()
        line[1]()
        if turn >= 1:
            lines[turn - 1][3]()
        if turn + 2 < one_items:
            depart(turn + 2)
        if turn >= 2:
            lines[turn - 2][4]()
        line[2]()
    lines[-1][3]()
    lines[-2][4]()
    lines[-1][4]()
    for line in lines:
        line[5]()

    @pl.when(lag > 0)
    def _():
        for item in range(one_items):
            shift(item).wait_send()


def scratch_of(items, lags, pars, members, sensors):
    width, share = sensors // items, sensors // pars
    quarter, groups = share // members, lags // members
    f32 = jnp.float32
    buffers = [
        pltpu.VMEM((items, pars, share, width), f32),
        pltpu.VMEM((items, max(pars - 1, 1), share, width), f32),
        pltpu.VMEM((items, members, quarter, width), f32),
        pltpu.VMEM((items, members, quarter, width), f32),
        pltpu.VMEM((items, quarter, width), f32),
        pltpu.VMEM((items, max(groups - 1, 1), quarter, width), f32),
        pltpu.VMEM((items, members, quarter, width), f32),
        pltpu.VMEM((items, members, quarter, width), f32),
    ]
    counts = (pars, pars, members, members, groups, groups, members, members)
    return buffers, tuple(pltpu.SemaphoreType.DMA((items, count)) for count in counts)


def solution(mesh):
    lags, pars = mesh.shape["lag"], mesh.shape["par"]

    def body(prior_rows, raw_rows):
        sensors, panel = prior_rows.shape[1:]
        share = sensors // pars
        members = group_size(lags, share)
        one_items = 4
        zero_buffers, zero_sems = scratch_of(1, lags, pars, members, sensors)
        one_buffers, one_sems = scratch_of(one_items, lags, pars, members, sensors)
        out = jax.ShapeDtypeStruct((1, share, sensors), jnp.float32)
        return pl.pallas_call(
            functools.partial(kernel, lags, pars, members, one_items),
            out_shape=(out, out),
            in_specs=[pl.BlockSpec(memory_space=pl.ANY)] * 2,
            out_specs=[pl.BlockSpec(memory_space=pltpu.VMEM)] * 2,
            scratch_shapes=[
                pltpu.VMEM((sensors, panel), jnp.bfloat16),
                pltpu.VMEM((sensors, panel), jnp.bfloat16),
                pltpu.VMEM((sensors, panel), jnp.bfloat16),
                *zero_buffers,
                *one_buffers,
                pltpu.SemaphoreType.DMA((2,)),
                pltpu.SemaphoreType.DMA((one_items,)),
                pltpu.SemaphoreType.DMA((one_items,)),
                zero_sems,
                one_sems,
            ],
            compiler_params=pltpu.CompilerParams(
                collective_id=0, has_side_effects=True, vmem_limit_bytes=60 * 2**20
            ),
            cost_estimate=pl.CostEstimate(
                flops=4 * sensors * sensors * panel,
                bytes_accessed=4 * sensors * panel + 8 * share * sensors,
                transcendentals=0,
            ),
        )(prior_rows, raw_rows)

    in_specs = (P("lag", None, "par"), P("lag", None, "par"))
    out_specs = (P("lag", "par", None), P("lag", "par", None))
    return jax.shard_map(body, mesh=mesh, in_specs=in_specs, out_specs=out_specs, check_vma=False)
```

time: 121 us -> 114 us (0.942)
  Pallas kernels: 115 us -> 109 us
    pallas_call x1, Pallas kernels: 115 us -> 109 us  [body(): pl.pallas_call(functools.partial(kernel, lags, pars, members, one_items),...]
    unnamed x6 -> x2, local copies, waits for them, and re-layouts: 4.76 us -> 3.74 us
where the time goes in v2:
time: 114 us; the launch traced here: 113 us
  Pallas kernels  109 us (96%)
  local copies, waits for them, and re-layouts  3.74 us (3%)
    pallas_call x1, Pallas kernels, body(): pl.pallas_call(functools.partial(kernel, lags, pars, members, one_items),...  109 us
    unnamed x2, local copies, waits for them, and re-layouts  3.74 us

profile of v2, /device:TPU:24, one launch (start us, length us, event | category | flops | bytes accessed | tf_op | source)
XLA Modules:
  0.0 113.4 jit_solution(348573264988250969)
XLA Ops:
  0.6 109.0 %shard_map.41 = (f32[1,256,512]{2,1,0:T(8,128)}, f32[1,256,512]{2,1,0:T(8,128)}) custom-call(bf16[1,512,2048]{2,1,0:T(8,128)(2,1)} %prior_hbm.1, bf16[1,512,2048]{2,1,0:T(8,128)(2,1)} %raw_hbm.1), custom_call_target="tpu_custom_call" | custom-call | flops 2147483648 | bytes 5242880 | tf_op jit(solution)/shard_map/pallas_call | solution.py:275
  109.7 1.9 %copy.6 = f32[1,256,512]{2,1,0:T(8,128)} copy(f32[1,256,512]{2,1,0:T(8,128)} %get-tuple-element.4) | data formatting | bytes 1048576
  111.5 1.9 %copy.7 = f32[1,256,512]{2,1,0:T(8,128)} copy(f32[1,256,512]{2,1,0:T(8,128)} %get-tuple-element.5) | data formatting | bytes 1048576

commit v3 on v2

--- a/solution.py
+++ b/solution.py
@@ -20,7 +20,7 @@
 
 
 def kernel(
-    lags, pars, members, one_items,
+    lags, pars, members, zero_items, one_items,
     prior_hbm, raw_hbm, zero_out, one_out,
     prior, raw, coming,
     zero_part, zero_met, zero_tile, zero_mates, zero_groups, zero_ahead, zero_first, zero_back,
@@ -51,19 +51,18 @@
         greet(lag, lax.rem(par + step, pars))
     for step in range(1, members):
         greet(base + lax.rem(member + step, members), par)
-    for step in range(1, groups):
-        greet(lax.rem(group + step, groups) * members + member, par)
-
-    @pl.when(lag > 0)
-    def _():
-        greet(lag - 1, par)
-
-    @pl.when(lag < lags - 1)
-    def _():
-        greet(lag + 1, par)
-
-    fixed = (pars - 1) + (members - 1) + (groups - 1)
-    pl.semaphore_wait(barrier, fixed + jnp.minimum(lag, 1) + jnp.minimum(lags - 1 - lag, 1))
+    met_by = (pars - 1) + (members - 1)
+    for reach in (1, members):
+        @pl.when(lag >= reach)
+        def _():
+            greet(lag - reach, par)
+
+        @pl.when(lag < lags - reach)
+        def _():
+            greet(lag + reach, par)
+
+        met_by = met_by + (lag >= reach).astype(jnp.int32) + (lag < lags - reach).astype(jnp.int32)
+    pl.semaphore_wait(barrier, met_by)
 
     span = raw.shape[0] // one_items
 
@@ -110,13 +109,13 @@
         gather = functools.partial(among, tile, mates, mate_send, mate_recv)
         give = functools.partial(among, first, back, back_send, back_recv)
 
-        def to_group(step):
+        def to_group():
             return pltpu.make_async_remote_copy(
                 src_ref=totals.at[item],
-                dst_ref=ahead.at[item, step - 1],
-                send_sem=group_send.at[item, step - 1],
-                recv_sem=group_recv.at[item, step - 1],
-                device_id=((group + step) * members + member, par),
+                dst_ref=ahead.at[item],
+                send_sem=group_send.at[item],
+                recv_sem=group_recv.at[item],
+                device_id=(lag + members, par),
                 device_id_type=MESH,
             )
 
@@ -141,27 +140,29 @@
                 gather(step, False).start()
             mates[item, member] = tile[item, member]
 
-        def sum_group():
+        def sum_before():
             for step in range(1, members):
                 gather(step, True).wait_recv()
-            total = mates[item, 0]
+
+            @pl.when(group == 0)
+            def _():
+                first[item, 0] = jnp.zeros_like(totals[item])
+
+            @pl.when(group > 0)
+            def _():
+                to_group().wait_recv()
+                first[item, 0] = ahead[item]
+
+            before = first[item, 0]
             for mate in range(1, members):
-                total = total + mates[item, mate]
-            totals[item] = total
-            for step in range(1, groups):
-                @pl.when(group + step < groups)
-                def _():
-                    to_group(step).start()
-
-        def sum_before():
-            first[item, 0] = jnp.zeros_like(totals[item])
-            for step in range(1, groups):
-                @pl.when(group >= step)
-                def _():
-                    to_group(step).wait_recv()
-                    first[item, 0] += ahead[item, step - 1]
-            for mate in range(1, members):
-                first[item, mate] = first[item, mate - 1] + mates[item, mate - 1]
+                before = before + mates[item, mate - 1]
+                first[item, mate] = before
+            totals[item] = before + mates[item, members - 1]
+
+            @pl.when(group < groups - 1)
+            def _():
+                to_group().start()
+
             for step in range(1, members):
                 give(step, False).start()
             back[item, member] = first[item, member]
@@ -180,12 +181,12 @@
             for step in range(1, members):
                 gather(step, False).wait_send()
                 give(step, False).wait_send()
-            for step in range(1, groups):
-                @pl.when(group + step < groups)
-                def _():
-                    to_group(step).wait_send()
-
-        return multiply, sum_peers, sum_group, sum_before, store, finish
+
+            @pl.when(group < groups - 1)
+            def _():
+                to_group().wait_send()
+
+        return multiply, sum_peers, sum_before, store, finish
 
     def arrive(item):
         @pl.when(lag < lags - 1)
@@ -202,10 +203,13 @@
         def _():
             shift(item).start()
 
-    zero = stages_of(
-        0, raw, zero_out, zero_part, zero_met, zero_tile, zero_mates,
-        zero_groups, zero_ahead, zero_first, zero_back, zero_sems,
-    )
+    zeros = [
+        stages_of(
+            item, raw, zero_out, zero_part, zero_met, zero_tile, zero_mates,
+            zero_groups, zero_ahead, zero_first, zero_back, zero_sems,
+        )
+        for item in range(zero_items)
+    ]
     ones = [
         stages_of(
             item, coming, one_out, one_part, one_met, one_tile, one_mates,
@@ -213,29 +217,26 @@
         )
         for item in range(one_items)
     ]
-    lines = [zero] + ones
-
-    depart(0)
-    depart(1)
+    lines = zeros + ones
+
+    for item in range(one_items):
+        depart(item)
     for load in loads:
         load.wait()
-    for turn, line in enumerate(lines):
-        if turn >= 1:
-            arrive(turn - 1)
-        line[0]()
-        line[1]()
-        if turn >= 1:
-            lines[turn - 1][3]()
-        if turn + 2 < one_items:
-            depart(turn + 2)
-        if turn >= 2:
-            lines[turn - 2][4]()
-        line[2]()
-    lines[-1][3]()
-    lines[-2][4]()
-    lines[-1][4]()
-    for line in lines:
-        line[5]()
+    for multiply, _, _, _, _ in zeros:
+        multiply()
+    for _, sum_peers, _, _, _ in zeros:
+        sum_peers()
+    for item, (multiply, sum_peers, _, _, _) in enumerate(ones):
+        arrive(item)
+        multiply()
+        sum_peers()
+    for _, _, sum_before, _, _ in lines:
+        sum_before()
+    for _, _, _, store, _ in lines:
+        store()
+    for _, _, _, _, finish in lines:
+        finish()
 
     @pl.when(lag > 0)
     def _():
@@ -245,7 +246,7 @@
 
 def scratch_of(items, lags, pars, members, sensors):
     width, share = sensors // items, sensors // pars
-    quarter, groups = share // members, lags // members
+    quarter = share // members
     f32 = jnp.float32
     buffers = [
         pltpu.VMEM((items, pars, share, width), f32),
@@ -253,12 +254,12 @@
         pltpu.VMEM((items, members, quarter, width), f32),
         pltpu.VMEM((items, members, quarter, width), f32),
         pltpu.VMEM((items, quarter, width), f32),
-        pltpu.VMEM((items, max(groups - 1, 1), quarter, width), f32),
+        pltpu.VMEM((items, quarter, width), f32),
         pltpu.VMEM((items, members, quarter, width), f32),
         pltpu.VMEM((items, members, quarter, width), f32),
     ]
-    counts = (pars, pars, members, members, groups, groups, members, members)
-    return buffers, tuple(pltpu.SemaphoreType.DMA((items, count)) for count in counts)
+    shapes = [(items, pars)] * 2 + [(items, members)] * 2 + [(items,)] * 2 + [(items, members)] * 2
+    return buffers, tuple(pltpu.SemaphoreType.DMA(shape) for shape in shapes)
 
 
 def solution(mesh):
@@ -268,12 +269,12 @@
         sensors, panel = prior_rows.shape[1:]
         share = sensors // pars
         members = group_size(lags, share)
-        one_items = 4
-        zero_buffers, zero_sems = scratch_of(1, lags, pars, members, sensors)
+        zero_items, one_items = 4, 4
+        zero_buffers, zero_sems = scratch_of(zero_items, lags, pars, members, sensors)
         one_buffers, one_sems = scratch_of(one_items, lags, pars, members, sensors)
         out = jax.ShapeDtypeStruct((1, share, sensors), jnp.float32)
         return pl.pallas_call(
-            functools.partial(kernel, lags, pars, members, one_items),
+            functools.partial(kernel, lags, pars, members, zero_items, one_items),
             out_shape=(out, out),
             in_specs=[pl.BlockSpec(memory_space=pl.ANY)] * 2,
             out_specs=[pl.BlockSpec(memory_space=pltpu.VMEM)] * 2,

time: 114 us -> 80.6 us (0.71)
  Pallas kernels: 109 us -> 75.1 us
    pallas_call x1, Pallas kernels: 109 us -> 75.1 us  [body(): pl.pallas_call(functools.partial(kernel, lags, pars, members, zero_items,...]
where the time goes in v3:
time: 80.6 us; the launch traced here: 79.4 us
  Pallas kernels  75.1 us (93%)
  local copies, waits for them, and re-layouts  3.74 us (5%)
    pallas_call x1, Pallas kernels, body(): pl.pallas_call(functools.partial(kernel, lags, pars, members, zero_items,...  75.1 us
    unnamed x2, local copies, waits for them, and re-layouts  3.74 us

profile of v3, /device:TPU:24, one launch (start us, length us, event | category | flops | bytes accessed | tf_op | source)
XLA Modules:
  0.0 79.4 jit_solution(7529724815740118629)
XLA Ops:
  0.6 75.1 %shard_map.41 = (f32[1,256,512]{2,1,0:T(8,128)}, f32[1,256,512]{2,1,0:T(8,128)}) custom-call(bf16[1,512,2048]{2,1,0:T(8,128)(2,1)} %prior_hbm.1, bf16[1,512,2048]{2,1,0:T(8,128)(2,1)} %raw_hbm.1), custom_call_target="tpu_custom_call" | custom-call | flops 2147483648 | bytes 5242880 | tf_op jit(solution)/shard_map/pallas_call | solution.py:276
  75.7 1.9 %copy.6 = f32[1,256,512]{2,1,0:T(8,128)} copy(f32[1,256,512]{2,1,0:T(8,128)} %get-tuple-element.4) | data formatting | bytes 1048576
  77.6 1.9 %copy.7 = f32[1,256,512]{2,1,0:T(8,128)} copy(f32[1,256,512]{2,1,0:T(8,128)} %get-tuple-element.5) | data formatting | bytes 1048576

commit v4 on v3

--- a/solution.py
+++ b/solution.py
@@ -231,7 +231,10 @@
         arrive(item)
         multiply()
         sum_peers()
-    for _, _, sum_before, _, _ in lines:
+        if item == one_items - 2:
+            for _, _, sum_before, _, _ in zeros:
+                sum_before()
+    for _, _, sum_before, _, _ in ones:
         sum_before()
     for _, _, _, store, _ in lines:
         store()
@@ -276,7 +279,7 @@
         return pl.pallas_call(
             functools.partial(kernel, lags, pars, members, zero_items, one_items),
             out_shape=(out, out),
-            in_specs=[pl.BlockSpec(memory_space=pl.ANY)] * 2,
+            in_specs=[pl.BlockSpec(memory_space=pltpu.HBM)] * 2,
             out_specs=[pl.BlockSpec(memory_space=pltpu.VMEM)] * 2,
             scratch_shapes=[
                 pltpu.VMEM((sensors, panel), jnp.bfloat16),
@@ -291,7 +294,7 @@
                 one_sems,
             ],
             compiler_params=pltpu.CompilerParams(
-                collective_id=0, has_side_effects=True, vmem_limit_bytes=60 * 2**20
+                collective_id=0, has_side_effects=True, vmem_limit_bytes=32 * 2**20
             ),
             cost_estimate=pl.CostEstimate(
                 flops=4 * sensors * sensors * panel,

time: 80.6 us -> 85.3 us (1.058); the launches traced: 79.4 us -> 85.1 us
  Pallas kernels: 75.1 us -> 79.7 us
  local copies, waits for them, and re-layouts: 3.74 us -> 4.76 us
    pallas_call x1, Pallas kernels: 75.1 us -> 79.7 us  [body(): pl.pallas_call(functools.partial(kernel, lags, pars, members, zero_items,...]
    unnamed x2 -> x6, local copies, waits for them, and re-layouts: 3.74 us -> 4.76 us
where the time goes in v4:
time: 85.3 us; the launch traced here: 85.1 us
  Pallas kernels  79.7 us (93%)
  local copies, waits for them, and re-layouts  4.76 us (6%)
    pallas_call x1, Pallas kernels, body(): pl.pallas_call(functools.partial(kernel, lags, pars, members, zero_items,...  79.7 us
    unnamed x6, local copies, waits for them, and re-layouts  4.76 us

profile of v4, /device:TPU:24, one launch (start us, length us, event | category | flops | bytes accessed | tf_op | source)
XLA Modules:
  0.0 85.1 jit_solution(6574397660879083516)
XLA Ops:
  0.6 0.0 copy-start
  0.6 1.6 %copy-done = bf16[1,512,2048]{2,1,0:T(8,128)(2,1)S(1)} copy-done((bf16[1,512,2048]{2,1,0:T(8,128)(2,1)S(1)}, bf16[1,512,2048]{2,1,0:T(8,128)(2,1)}, u32[]{:S(2)}) %copy-start) | copy-done | bytes 2097176
  2.2 0.0 copy-start.1
  2.2 1.6 %copy-done.1 = bf16[1,512,2048]{2,1,0:T(8,128)(2,1)S(1)} copy-done((bf16[1,512,2048]{2,1,0:T(8,128)(2,1)S(1)}, bf16[1,512,2048]{2,1,0:T(8,128)(2,1)}, u32[]{:S(2)}) %copy-start.1) | copy-done | bytes 2097176
  3.8 79.7 %shard_map.41 = (f32[1,256,512]{2,1,0:T(8,128)S(1)}, f32[1,256,512]{2,1,0:T(8,128)S(1)}) custom-call(bf16[1,512,2048]{2,1,0:T(8,128)(2,1)S(1)} %copy-done, bf16[1,512,2048]{2,1,0:T(8,128)(2,1)S(1)} %copy-done.1), custom_call_target="tpu_custom_call" | custom-call | flops 2147483648 | bytes 5242880 | tf_op jit(solution)/shard_map/pallas_call | solution.py:279
  83.5 0.8 copy.6
  84.3 0.8 copy.7
Async XLA Ops:
  0.6 1.6 %copy-start = (bf16[1,512,2048]{2,1,0:T(8,128)(2,1)S(1)}, bf16[1,512,2048]{2,1,0:T(8,128)(2,1)}, u32[]{:S(2)}) copy-start(bf16[1,512,2048]{2,1,0:T(8,128)(2,1)} %prior_hbm.1) | copy-start | bytes 6291460
  2.2 1.6 %copy-start.1 = (bf16[1,512,2048]{2,1,0:T(8,128)(2,1)S(1)}, bf16[1,512,2048]{2,1,0:T(8,128)(2,1)}, u32[]{:S(2)}) copy-start(bf16[1,512,2048]{2,1,0:T(8,128)(2,1)} %raw_hbm.1) | copy-start | bytes 6291460

commit v5 on v3

--- a/solution.py
+++ b/solution.py
@@ -8,7 +8,25 @@
 from jax.sharding import PartitionSpec as P
 
 MESH = pl.DeviceIdType.MESH
-SENT = jnp.float32
+TOP = 240.0
+
+
+def coded(values):
+    scale = jnp.max(jnp.abs(values), axis=0, keepdims=True)
+    power = values * (TOP / jnp.maximum(scale, 1e-36))
+    negative = power < 0
+    for _ in range(4):
+        power = power * power
+    return jnp.where(negative, -power, power).astype(jnp.bfloat16), scale * (1.0 / TOP)
+
+
+def decoded(code, scale):
+    code = code.astype(jnp.float32)
+    root = jnp.maximum(jnp.abs(code), 2e-38)
+    for _ in range(4):
+        root = lax.rsqrt(root)
+    root = root * scale
+    return jnp.where(code == 0, 0.0, jnp.where(code < 0, -root, root))
 
 
 def group_size(lags, rows):
@@ -23,8 +41,7 @@
     lags, pars, members, zero_items, one_items,
     prior_hbm, raw_hbm, zero_out, one_out,
     prior, raw, coming,
-    zero_part, zero_met, zero_tile, zero_mates, zero_groups, zero_ahead, zero_first, zero_back,
-    one_part, one_met, one_tile, one_mates, one_groups, one_ahead, one_first, one_back,
+    zero_buffers, one_buffers,
     load_sem, shift_send, shift_recv,
     zero_sems, one_sems,
 ):
@@ -77,8 +94,11 @@
             device_id_type=MESH,
         )
 
-    def stages_of(item, rows_ref, out_ref, part, met, tile, mates, totals, ahead, first, back, sems):
-        (part_send, part_recv, mate_send, mate_recv, group_send, group_recv, back_send, back_recv) = sems
+    def stages_of(item, rows_ref, out_ref, buffers, sems):
+        (part, met, tile, mates, totals, ahead, first, back) = buffers[:8]
+        (tile_code, tile_scale, mates_code, mates_scale) = buffers[8:12]
+        (first_code, first_scale, back_code, back_scale) = buffers[12:]
+        (part_send, part_recv, group_send, group_recv) = sems[:4]
         width = part.shape[-1]
         share = part.shape[2]
         quarter = tile.shape[2]
@@ -106,8 +126,21 @@
                 device_id_type=MESH,
             )
 
-        gather = functools.partial(among, tile, mates, mate_send, mate_recv)
-        give = functools.partial(among, first, back, back_send, back_recv)
+        gather = [
+            functools.partial(among, tile_code, mates_code, sems[4], sems[5]),
+            functools.partial(among, tile_scale, mates_scale, sems[6], sems[7]),
+        ]
+        give = [
+            functools.partial(among, first_code, back_code, sems[8], sems[9]),
+            functools.partial(among, first_scale, back_scale, sems[10], sems[11]),
+        ]
+
+        def receive(kinds, code, scale, target):
+            for step in range(1, members):
+                for kind in kinds:
+                    kind(step, True).wait_recv()
+                mate = lax.rem(member + step, members)
+                target[item, mate] = decoded(code[item, mate], scale[item, mate])
 
         def to_group():
             return pltpu.make_async_remote_copy(
@@ -135,14 +168,16 @@
                 to_peer(step).wait_recv()
                 total = total + met[item, step - 1]
             for owner in range(members):
-                tile[item, owner] = total[owner * quarter:(owner + 1) * quarter]
+                rows = total[owner * quarter:(owner + 1) * quarter]
+                tile[item, owner] = rows
+                tile_code[item, owner], tile_scale[item, owner] = coded(rows)
             for step in range(1, members):
-                gather(step, False).start()
+                for kind in gather:
+                    kind(step, False).start()
             mates[item, member] = tile[item, member]
 
         def sum_before():
-            for step in range(1, members):
-                gather(step, True).wait_recv()
+            receive(gather, mates_code, mates_scale, mates)
 
             @pl.when(group == 0)
             def _():
@@ -163,13 +198,15 @@
             def _():
                 to_group().start()
 
+            for mate in range(members):
+                first_code[item, mate], first_scale[item, mate] = coded(first[item, mate])
             for step in range(1, members):
-                give(step, False).start()
+                for kind in give:
+                    kind(step, False).start()
             back[item, member] = first[item, member]
 
         def store():
-            for step in range(1, members):
-                give(step, True).wait_recv()
+            receive(give, back_code, back_scale, back)
             for owner in range(members):
                 out_ref[0, owner * quarter:(owner + 1) * quarter, item * width:(item + 1) * width] = (
                     back[item, owner] + tile[item, owner]
@@ -179,8 +216,8 @@
             for step in range(1, pars):
                 to_peer(step).wait_send()
             for step in range(1, members):
-                gather(step, False).wait_send()
-                give(step, False).wait_send()
+                for kind in gather + give:
+                    kind(step, False).wait_send()
 
             @pl.when(group < groups - 1)
             def _():
@@ -204,18 +241,10 @@
             shift(item).start()
 
     zeros = [
-        stages_of(
-            item, raw, zero_out, zero_part, zero_met, zero_tile, zero_mates,
-            zero_groups, zero_ahead, zero_first, zero_back, zero_sems,
-        )
-        for item in range(zero_items)
+        stages_of(item, raw, zero_out, zero_buffers, zero_sems) for item in range(zero_items)
     ]
     ones = [
-        stages_of(
-            item, coming, one_out, one_part, one_met, one_tile, one_mates,
-            one_groups, one_ahead, one_first, one_back, one_sems,
-        )
-        for item in range(one_items)
+        stages_of(item, coming, one_out, one_buffers, one_sems) for item in range(one_items)
     ]
     lines = zeros + ones
 
@@ -258,8 +287,11 @@
         pltpu.VMEM((items, members, quarter, width), f32),
         pltpu.VMEM((items, members, quarter, width), f32),
     ]
-    shapes = [(items, pars)] * 2 + [(items, members)] * 2 + [(items,)] * 2 + [(items, members)] * 2
-    return buffers, tuple(pltpu.SemaphoreType.DMA(shape) for shape in shapes)
+    for _ in range(4):
+        buffers.append(pltpu.VMEM((items, members, quarter, width), jnp.bfloat16))
+        buffers.append(pltpu.VMEM((items, members, 1, width), f32))
+    shapes = [(items, pars)] * 2 + [(items,)] * 2 + [(items, members)] * 8
+    return tuple(buffers), tuple(pltpu.SemaphoreType.DMA(shape) for shape in shapes)
 
 
 def solution(mesh):
@@ -269,7 +301,7 @@
         sensors, panel = prior_rows.shape[1:]
         share = sensors // pars
         members = group_size(lags, share)
-        zero_items, one_items = 4, 4
+        zero_items, one_items = 2, 4
         zero_buffers, zero_sems = scratch_of(zero_items, lags, pars, members, sensors)
         one_buffers, one_sems = scratch_of(one_items, lags, pars, members, sensors)
         out = jax.ShapeDtypeStruct((1, share, sensors), jnp.float32)
@@ -282,8 +314,8 @@
                 pltpu.VMEM((sensors, panel), jnp.bfloat16),
                 pltpu.VMEM((sensors, panel), jnp.bfloat16),
                 pltpu.VMEM((sensors, panel), jnp.bfloat16),
-                *zero_buffers,
-                *one_buffers,
+                zero_buffers,
+                one_buffers,
                 pltpu.SemaphoreType.DMA((2,)),
                 pltpu.SemaphoreType.DMA((one_items,)),
                 pltpu.SemaphoreType.DMA((one_items,)),
@@ -291,7 +323,7 @@
                 one_sems,
             ],
             compiler_params=pltpu.CompilerParams(
-                collective_id=0, has_side_effects=True, vmem_limit_bytes=60 * 2**20
+                collective_id=0, has_side_effects=True, vmem_limit_bytes=52 * 2**20
             ),
             cost_estimate=pl.CostEstimate(
                 flops=4 * sensors * sensors * panel,

time: 80.6 us -> 73.9 us (0.917); the launches traced: 79.4 us -> 73.8 us
  Pallas kernels: 75.1 us -> 71.5 us
  local copies, waits for them, and re-layouts: 3.74 us -> 1.59 us
    pallas_call x1, Pallas kernels: 75.1 us -> 71.5 us  [body(): pl.pallas_call(functools.partial(kernel, lags, pars, members, zero_items,...]
    unnamed x2, local copies, waits for them, and re-layouts: 3.74 us -> 1.59 us
where the time goes in v5:
time: 73.9 us; the launch traced here: 73.8 us
  Pallas kernels  71.5 us (97%)
  local copies, waits for them, and re-layouts  1.59 us (2%)
    pallas_call x1, Pallas kernels, body(): pl.pallas_call(functools.partial(kernel, lags, pars, members, zero_items,...  71.5 us
    unnamed x2, local copies, waits for them, and re-layouts  1.59 us

profile of v5, /device:TPU:24, one launch (start us, length us, event | category | flops | bytes accessed | tf_op | source)
XLA Modules:
  0.0 73.8 jit_solution(4076598968800472709)
XLA Ops:
  0.6 71.5 %shard_map.41 = (f32[1,256,512]{2,1,0:T(8,128)S(1)}, f32[1,256,512]{2,1,0:T(8,128)S(1)}) custom-call(bf16[1,512,2048]{2,1,0:T(8,128)(2,1)} %prior_hbm.1, bf16[1,512,2048]{2,1,0:T(8,128)(2,1)} %raw_hbm.1), custom_call_target="tpu_custom_call" | custom-call | flops 2147483648 | bytes 5242880 | tf_op jit(solution)/shard_map/pallas_call | solution.py:308
  72.2 0.8 %copy.6 = f32[1,256,512]{2,1,0:T(8,128)} copy(f32[1,256,512]{2,1,0:T(8,128)S(1)} %get-tuple-element.4) | data formatting | bytes 1048576
  73.0 0.8 %copy.7 = f32[1,256,512]{2,1,0:T(8,128)} copy(f32[1,256,512]{2,1,0:T(8,128)S(1)} %get-tuple-element.5) | data formatting | bytes 1048576

commit v6 on v5

--- a/solution.py
+++ b/solution.py
@@ -69,7 +69,7 @@
     for step in range(1, members):
         greet(base + lax.rem(member + step, members), par)
     met_by = (pars - 1) + (members - 1)
-    for reach in (1, members):
+    for reach in [1] + [members * step for step in range(1, groups)]:
         @pl.when(lag >= reach)
         def _():
             greet(lag - reach, par)
@@ -94,7 +94,7 @@
             device_id_type=MESH,
         )
 
-    def stages_of(item, rows_ref, out_ref, buffers, sems):
+    def stages_of(item, rows_ref, out_ref, buffers, sems, reaches):
         (part, met, tile, mates, totals, ahead, first, back) = buffers[:8]
         (tile_code, tile_scale, mates_code, mates_scale) = buffers[8:12]
         (first_code, first_scale, back_code, back_scale) = buffers[12:]
@@ -142,13 +142,13 @@
                 mate = lax.rem(member + step, members)
                 target[item, mate] = decoded(code[item, mate], scale[item, mate])
 
-        def to_group():
+        def to_group(reach):
             return pltpu.make_async_remote_copy(
                 src_ref=totals.at[item],
-                dst_ref=ahead.at[item],
-                send_sem=group_send.at[item],
-                recv_sem=group_recv.at[item],
-                device_id=(lag + members, par),
+                dst_ref=ahead.at[item, reach - 1],
+                send_sem=group_send.at[item, reach - 1],
+                recv_sem=group_recv.at[item, reach - 1],
+                device_id=(lag + reach * members, par),
                 device_id_type=MESH,
             )
 
@@ -178,26 +178,33 @@
 
         def sum_before():
             receive(gather, mates_code, mates_scale, mates)
-
-            @pl.when(group == 0)
-            def _():
-                first[item, 0] = jnp.zeros_like(totals[item])
-
-            @pl.when(group > 0)
-            def _():
-                to_group().wait_recv()
-                first[item, 0] = ahead[item]
-
+            own = mates[item, 0]
+            for mate in range(1, members):
+                own = own + mates[item, mate]
+
+            def send():
+                for reach in reaches:
+                    @pl.when(group + reach < groups)
+                    def _():
+                        to_group(reach).start()
+
+            chained = len(reaches) == 1
+            if not chained:
+                totals[item] = own
+                send()
+            first[item, 0] = jnp.zeros_like(own)
+            for reach in reaches:
+                @pl.when(group >= reach)
+                def _():
+                    to_group(reach).wait_recv()
+                    first[item, 0] += ahead[item, reach - 1]
             before = first[item, 0]
+            if chained:
+                totals[item] = before + own
+                send()
             for mate in range(1, members):
                 before = before + mates[item, mate - 1]
                 first[item, mate] = before
-            totals[item] = before + mates[item, members - 1]
-
-            @pl.when(group < groups - 1)
-            def _():
-                to_group().start()
-
             for mate in range(members):
                 first_code[item, mate], first_scale[item, mate] = coded(first[item, mate])
             for step in range(1, members):
@@ -219,9 +226,10 @@
                 for kind in gather + give:
                     kind(step, False).wait_send()
 
-            @pl.when(group < groups - 1)
-            def _():
-                to_group().wait_send()
+            for reach in reaches:
+                @pl.when(group + reach < groups)
+                def _():
+                    to_group(reach).wait_send()
 
         return multiply, sum_peers, sum_before, store, finish
 
@@ -241,14 +249,21 @@
             shift(item).start()
 
     zeros = [
-        stages_of(item, raw, zero_out, zero_buffers, zero_sems) for item in range(zero_items)
+        stages_of(item, raw, zero_out, zero_buffers, zero_sems, (1,)) for item in range(zero_items)
     ]
     ones = [
-        stages_of(item, coming, one_out, one_buffers, one_sems) for item in range(one_items)
+        stages_of(item, coming, one_out, one_buffers, one_sems, range(1, groups))
+        for item in range(one_items)
     ]
     lines = zeros + ones
-
-    for item in range(one_items):
+    last = one_items - 1
+
+    def work_on(item):
+        arrive(item)
+        ones[item][0]()
+        ones[item][1]()
+
+    for item in range(last - 1):
         depart(item)
     for load in loads:
         load.wait()
@@ -256,13 +271,21 @@
         multiply()
     for _, sum_peers, _, _, _ in zeros:
         sum_peers()
-    for item, (multiply, sum_peers, _, _, _) in enumerate(ones):
-        arrive(item)
-        multiply()
-        sum_peers()
-    for _, _, sum_before, _, _ in lines:
+    depart(last - 1)
+    for item in range(last - 1):
+        work_on(item)
+    zeros[0][2]()
+    depart(last)
+    for _, _, sum_before, _, _ in zeros[1:]:
         sum_before()
-    for _, _, _, store, _ in lines:
+    work_on(last - 1)
+    for _, _, sum_before, _, _ in ones[:last - 1]:
+        sum_before()
+    zeros[0][3]()
+    work_on(last)
+    for _, _, sum_before, _, _ in ones[last - 1:]:
+        sum_before()
+    for _, _, _, store, _ in lines[1:]:
         store()
     for _, _, _, _, finish in lines:
         finish()
@@ -273,7 +296,7 @@
             shift(item).wait_send()
 
 
-def scratch_of(items, lags, pars, members, sensors):
+def scratch_of(items, lags, pars, members, reached, sensors):
     width, share = sensors // items, sensors // pars
     quarter = share // members
     f32 = jnp.float32
@@ -283,14 +306,14 @@
         pltpu.VMEM((items, members, quarter, width), f32),
         pltpu.VMEM((items, members, quarter, width), f32),
         pltpu.VMEM((items, quarter, width), f32),
-        pltpu.VMEM((items, quarter, width), f32),
+        pltpu.VMEM((items, reached, quarter, width), f32),
         pltpu.VMEM((items, members, quarter, width), f32),
         pltpu.VMEM((items, members, quarter, width), f32),
     ]
     for _ in range(4):
         buffers.append(pltpu.VMEM((items, members, quarter, width), jnp.bfloat16))
         buffers.append(pltpu.VMEM((items, members, 1, width), f32))
-    shapes = [(items, pars)] * 2 + [(items,)] * 2 + [(items, members)] * 8
+    shapes = [(items, pars)] * 2 + [(items, reached)] * 2 + [(items, members)] * 8
     return tuple(buffers), tuple(pltpu.SemaphoreType.DMA(shape) for shape in shapes)
 
 
@@ -302,8 +325,8 @@
         share = sensors // pars
         members = group_size(lags, share)
         zero_items, one_items = 2, 4
-        zero_buffers, zero_sems = scratch_of(zero_items, lags, pars, members, sensors)
-        one_buffers, one_sems = scratch_of(one_items, lags, pars, members, sensors)
+        zero_buffers, zero_sems = scratch_of(zero_items, lags, pars, members, 1, sensors)
+        one_buffers, one_sems = scratch_of(one_items, lags, pars, members, max(lags // members - 1, 1), sensors)
         out = jax.ShapeDtypeStruct((1, share, sensors), jnp.float32)
         return pl.pallas_call(
             functools.partial(kernel, lags, pars, members, zero_items, one_items),

time: 73.9 us -> 89 us (1.20)
  Pallas kernels: 71.5 us -> 86.6 us
    pallas_call x1, Pallas kernels: 71.5 us -> 86.6 us  [body(): pl.pallas_call(functools.partial(kernel, lags, pars, members, zero_items,...]
where the time goes in v6:
time: 89 us; the launch traced here: 88.8 us
  Pallas kernels  86.6 us (97%)
  local copies, waits for them, and re-layouts  1.59 us (2%)
    pallas_call x1, Pallas kernels, body(): pl.pallas_call(functools.partial(kernel, lags, pars, members, zero_items,...  86.6 us

profile of v6, /device:TPU:24, one launch (start us, length us, event | category | flops | bytes accessed | tf_op | source)
XLA Modules:
  0.0 88.8 jit_solution(9374847125945951026)
XLA Ops:
  0.6 86.6 %shard_map.41 = (f32[1,256,512]{2,1,0:T(8,128)S(1)}, f32[1,256,512]{2,1,0:T(8,128)S(1)}) custom-call(bf16[1,512,2048]{2,1,0:T(8,128)(2,1)} %prior_hbm.1, bf16[1,512,2048]{2,1,0:T(8,128)(2,1)} %raw_hbm.1), custom_call_target="tpu_custom_call" | custom-call | flops 2147483648 | bytes 5242880 | tf_op jit(solution)/shard_map/pallas_call | solution.py:331
  87.3 0.8 copy.6
  88.0 0.8 copy.7

commit v7 on v6

--- a/solution.py
+++ b/solution.py
@@ -259,7 +259,6 @@
     last = one_items - 1
 
     def work_on(item):
-        arrive(item)
         ones[item][0]()
         ones[item][1]()
 
@@ -272,21 +271,26 @@
     for _, sum_peers, _, _, _ in zeros:
         sum_peers()
     depart(last - 1)
+    for _, _, sum_before, _, _ in zeros:
+        sum_before()
+    for item in range(last - 1):
+        arrive(item)
+    depart(last)
     for item in range(last - 1):
         work_on(item)
-    zeros[0][2]()
-    depart(last)
-    for _, _, sum_before, _, _ in zeros[1:]:
+    for _, _, _, store, _ in zeros:
+        store()
+    arrive(last - 1)
+    work_on(last - 1)
+    for _, _, sum_before, _, _ in ones[:last]:
         sum_before()
-    work_on(last - 1)
-    for _, _, sum_before, _, _ in ones[:last - 1]:
-        sum_before()
-    zeros[0][3]()
+    for _, _, _, store, _ in ones[:last - 1]:
+        store()
+    arrive(last)
     work_on(last)
-    for _, _, sum_before, _, _ in ones[last - 1:]:
-        sum_before()
-    for _, _, _, store, _ in lines[1:]:
-        store()
+    ones[last][2]()
+    ones[last - 1][3]()
+    ones[last][3]()
     for _, _, _, _, finish in lines:
         finish()
 

time: 89 us -> 96.9 us (1.089)
  Pallas kernels: 86.6 us -> 94.4 us
    pallas_call x1, Pallas kernels: 86.6 us -> 94.4 us  [body(): pl.pallas_call(functools.partial(kernel, lags, pars, members, zero_items,...]
where the time goes in v7:
time: 96.9 us; the launch traced here: 96.7 us
  Pallas kernels  94.4 us (97%)
  local copies, waits for them, and re-layouts  1.59 us (2%)
    pallas_call x1, Pallas kernels, body(): pl.pallas_call(functools.partial(kernel, lags, pars, members, zero_items,...  94.4 us

profile of v7, /device:TPU:24, one launch (start us, length us, event | category | flops | bytes accessed | tf_op | source)
XLA Modules:
  0.0 96.7 jit_solution(3163963111415866095)
XLA Ops:
  0.6 94.4 %shard_map.41 = (f32[1,256,512]{2,1,0:T(8,128)S(1)}, f32[1,256,512]{2,1,0:T(8,128)S(1)}) custom-call(bf16[1,512,2048]{2,1,0:T(8,128)(2,1)} %prior_hbm.1, bf16[1,512,2048]{2,1,0:T(8,128)(2,1)} %raw_hbm.1), custom_call_target="tpu_custom_call" | custom-call | flops 2147483648 | bytes 5242880 | tf_op jit(solution)/shard_map/pallas_call | solution.py:335
  95.1 0.8 copy.6
  95.9 0.8 copy.7

commit v8 on v5

--- a/solution.py
+++ b/solution.py
@@ -248,17 +248,27 @@
     ]
     lines = zeros + ones
 
-    for item in range(one_items):
+    last = one_items - 1
+    for item in range(last - 1):
         depart(item)
     for load in loads:
         load.wait()
     for multiply, _, _, _, _ in zeros:
         multiply()
+    depart(last - 1)
+    for item in range(last - 1):
+        arrive(item)
+        ones[item][0]()
     for _, sum_peers, _, _, _ in zeros:
         sum_peers()
-    for item, (multiply, sum_peers, _, _, _) in enumerate(ones):
-        arrive(item)
-        multiply()
+    depart(last)
+    arrive(last - 1)
+    ones[last - 1][0]()
+    for _, sum_peers, _, _, _ in ones[:last - 1]:
+        sum_peers()
+    arrive(last)
+    ones[last][0]()
+    for _, sum_peers, _, _, _ in ones[last - 1:]:
         sum_peers()
     for _, _, sum_before, _, _ in lines:
         sum_before()

time: 73.9 us -> 76.6 us (1.037)
  Pallas kernels: 71.5 us -> 74.3 us
    pallas_call x1, Pallas kernels: 71.5 us -> 74.3 us  [body(): pl.pallas_call(functools.partial(kernel, lags, pars, members, zero_items,...]
where the time goes in v8:
time: 76.6 us; the launch traced here: 76.5 us
  Pallas kernels  74.3 us (97%)
  local copies, waits for them, and re-layouts  1.59 us (2%)
    pallas_call x1, Pallas kernels, body(): pl.pallas_call(functools.partial(kernel, lags, pars, members, zero_items,...  74.3 us
    unnamed x2, local copies, waits for them, and re-layouts  1.59 us

profile of v8, /device:TPU:24, one launch (start us, length us, event | category | flops | bytes accessed | tf_op | source)
XLA Modules:
  0.0 76.5 jit_solution(4463961444104938729)
XLA Ops:
  0.6 74.3 %shard_map.41 = (f32[1,256,512]{2,1,0:T(8,128)S(1)}, f32[1,256,512]{2,1,0:T(8,128)S(1)}) custom-call(bf16[1,512,2048]{2,1,0:T(8,128)(2,1)} %prior_hbm.1, bf16[1,512,2048]{2,1,0:T(8,128)(2,1)} %raw_hbm.1), custom_call_target="tpu_custom_call" | custom-call | flops 2147483648 | bytes 5242880 | tf_op jit(solution)/shard_map/pallas_call | solution.py:318
  74.9 0.8 %copy.6 = f32[1,256,512]{2,1,0:T(8,128)} copy(f32[1,256,512]{2,1,0:T(8,128)S(1)} %get-tuple-element.4) | data formatting | bytes 1048576
  75.7 0.8 %copy.7 = f32[1,256,512]{2,1,0:T(8,128)} copy(f32[1,256,512]{2,1,0:T(8,128)S(1)} %get-tuple-element.5) | data formatting | bytes 1048576

commit v9 on v5

--- a/solution.py
+++ b/solution.py
@@ -254,11 +254,10 @@
         load.wait()
     for multiply, _, _, _, _ in zeros:
         multiply()
-    for _, sum_peers, _, _, _ in zeros:
-        sum_peers()
-    for item, (multiply, sum_peers, _, _, _) in enumerate(ones):
+    for item, (multiply, _, _, _, _) in enumerate(ones):
         arrive(item)
         multiply()
+    for _, sum_peers, _, _, _ in lines:
         sum_peers()
     for _, _, sum_before, _, _ in lines:
         sum_before()

time: 73.9 us -> 75.7 us (1.024)
  Pallas kernels: 71.5 us -> 73.3 us
    pallas_call x1, Pallas kernels: 71.5 us -> 73.3 us  [body(): pl.pallas_call(functools.partial(kernel, lags, pars, members, zero_items,...]
where the time goes in v9:
time: 75.7 us; the launch traced here: 75.5 us
  Pallas kernels  73.3 us (97%)
  local copies, waits for them, and re-layouts  1.59 us (2%)
    pallas_call x1, Pallas kernels, body(): pl.pallas_call(functools.partial(kernel, lags, pars, members, zero_items,...  73.3 us
    unnamed x2, local copies, waits for them, and re-layouts  1.59 us

profile of v9, /device:TPU:24, one launch (start us, length us, event | category | flops | bytes accessed | tf_op | source)
XLA Modules:
  0.0 75.5 jit_solution(17159304404062153028)
XLA Ops:
  0.6 73.3 %shard_map.41 = (f32[1,256,512]{2,1,0:T(8,128)S(1)}, f32[1,256,512]{2,1,0:T(8,128)S(1)}) custom-call(bf16[1,512,2048]{2,1,0:T(8,128)(2,1)} %prior_hbm.1, bf16[1,512,2048]{2,1,0:T(8,128)(2,1)} %raw_hbm.1), custom_call_target="tpu_custom_call" | custom-call | flops 2147483648 | bytes 5242880 | tf_op jit(solution)/shard_map/pallas_call | solution.py:307
  73.9 0.8 %copy.6 = f32[1,256,512]{2,1,0:T(8,128)} copy(f32[1,256,512]{2,1,0:T(8,128)S(1)} %get-tuple-element.4) | data formatting | bytes 1048576
  74.7 0.8 %copy.7 = f32[1,256,512]{2,1,0:T(8,128)} copy(f32[1,256,512]{2,1,0:T(8,128)S(1)} %get-tuple-element.5) | data formatting | bytes 1048576

commit v10 on v5

--- a/solution.py
+++ b/solution.py
@@ -176,28 +176,34 @@
                     kind(step, False).start()
             mates[item, member] = tile[item, member]
 
-        def sum_before():
+        def gather_tiles():
             receive(gather, mates_code, mates_scale, mates)
+
+        def sum_groups():
+            own = mates[item, 0]
+            for mate in range(1, members):
+                own = own + mates[item, mate]
 
             @pl.when(group == 0)
             def _():
-                first[item, 0] = jnp.zeros_like(totals[item])
+                first[item, 0] = jnp.zeros_like(own)
 
             @pl.when(group > 0)
             def _():
                 to_group().wait_recv()
                 first[item, 0] = ahead[item]
 
+            totals[item] = first[item, 0] + own
+
+            @pl.when(group < groups - 1)
+            def _():
+                to_group().start()
+
+        def sum_before():
             before = first[item, 0]
             for mate in range(1, members):
                 before = before + mates[item, mate - 1]
                 first[item, mate] = before
-            totals[item] = before + mates[item, members - 1]
-
-            @pl.when(group < groups - 1)
-            def _():
-                to_group().start()
-
             for mate in range(members):
                 first_code[item, mate], first_scale[item, mate] = coded(first[item, mate])
             for step in range(1, members):
@@ -223,7 +229,7 @@
             def _():
                 to_group().wait_send()
 
-        return multiply, sum_peers, sum_before, store, finish
+        return multiply, sum_peers, (gather_tiles, sum_groups, sum_before), store, finish
 
     def arrive(item):
         @pl.when(lag < lags - 1)
@@ -260,8 +266,9 @@
         arrive(item)
         multiply()
         sum_peers()
-    for _, _, sum_before, _, _ in lines:
-        sum_before()
+    for stage in range(3):
+        for _, _, prefix, _, _ in lines:
+            prefix[stage]()
     for _, _, _, store, _ in lines:
         store()
     for _, _, _, _, finish in lines:

time: 73.9 us -> 80 us (1.083)
  Pallas kernels: 71.5 us -> 77.6 us
    pallas_call x1, Pallas kernels: 71.5 us -> 77.6 us  [body(): pl.pallas_call(functools.partial(kernel, lags, pars, members, zero_items,...]
where the time goes in v10:
time: 80 us; the launch traced here: 79.8 us
  Pallas kernels  77.6 us (97%)
  local copies, waits for them, and re-layouts  1.59 us (2%)
    pallas_call x1, Pallas kernels, body(): pl.pallas_call(functools.partial(kernel, lags, pars, members, zero_items,...  77.6 us

profile of v10, /device:TPU:24, one launch (start us, length us, event | category | flops | bytes accessed | tf_op | source)
XLA Modules:
  0.0 79.8 jit_solution(5524232091183656817)
XLA Ops:
  0.6 77.6 %shard_map.41 = (f32[1,256,512]{2,1,0:T(8,128)S(1)}, f32[1,256,512]{2,1,0:T(8,128)S(1)}) custom-call(bf16[1,512,2048]{2,1,0:T(8,128)(2,1)} %prior_hbm.1, bf16[1,512,2048]{2,1,0:T(8,128)(2,1)} %raw_hbm.1), custom_call_target="tpu_custom_call" | custom-call | flops 2147483648 | bytes 5242880 | tf_op jit(solution)/shard_map/pallas_call | solution.py:315
  78.2 0.8 copy.6
  79.0 0.8 copy.7
